TPU v7x, 32 devices: a whole 2x2x4 slice. The times are simulated.
32 devices in a mesh: dom: 4 (over y, x), grp: 8 (over z, core).
Axes of the slice: x: 2, y: 2, z: 4, core: 2. Of those that a mesh axis runs over, the one named last changes fastest.
Arguments:
- features: bfloat16 [8192, 256], P(('dom', 'grp')), may hold values from -6 to 6
- adjacency: bfloat16 [512, 128, 128], P(('dom', 'grp')), may hold values from -0.1875 to 0.1875
- src_tile: int32 [512], P(('dom', 'grp')), may hold values from 0 to 1
- dst_peer: int32 [512, 1], P(('dom', 'grp')), may hold values from 0 to 3; in each aligned block of 16 rows (0 to 15, 16 to 31, ...) at most 8 rows name the same one
- dst_tile: int32 [512], P(('dom', 'grp')), may hold values from 0 to 1
- w_self: bfloat16 [256, 256], replicated, may hold values from -0.375 to 0.375
- w_neigh: bfloat16 [256, 256], replicated, may hold values from -0.375 to 0.375
- out_grad: bfloat16 [8192, 256], P(('dom', 'grp')), may hold values from -6 to 6
Outputs:
- output: bfloat16 [8192, 256], P(('dom', 'grp'))
- feat_grad: bfloat16 [8192, 256], P(('dom', 'grp'))
- weight_grads: float32 [2, 256, 256], replicated
Inputs may be any that keep to these rules, and one draw needn't show every extreme that they name: `dst_peer`: among the 16 blocks of one device no partition is named more than 8 times, a bound that some block reaches.
All inputs are finite; a program needn't handle non-finite values.
Results may differ from a plain program's by a relative error of at most 0.015.
Values may be sent and summed in bfloat16 or wider, within the bound.
A program may use at most 64 MiB of HBM per device.

v0:
```python
import math

import jax
import jax.numpy as jnp
from jax import lax
from jax.sharding import PartitionSpec as P


def body(features, adjacency, src_tile, dst_peer, dst_tile, w_self, w_neigh, out_grad):
    nodes, width = features.shape
    tile = adjacency.shape[1]
    n_tiles = nodes // tile
    parts = lax.axis_size("dom")
    blocks = features.reshape(n_tiles, tile, width)
    products = jnp.einsum(
        "tij,tjf->tif", adjacency, blocks[src_tile], preferred_element_type=jnp.float32
    ).astype(jnp.bfloat16)
    peers = dst_peer[:, 0]
    target = peers * n_tiles + dst_tile
    dense = (
        jnp.zeros((parts * n_tiles, tile, width), jnp.float32)
        .at[target]
        .add(products.astype(jnp.float32))
    )
    flat = dense.reshape(parts * nodes, width)
    agg = lax.psum_scatter(flat, "dom", scatter_dimension=0, tiled=True)
    agg_low = agg.astype(jnp.bfloat16)
    pre = jnp.dot(features, w_self, preferred_element_type=jnp.float32) + jnp.dot(
        agg_low, w_neigh, preferred_element_type=jnp.float32
    )
    sig = jax.nn.sigmoid(pre)
    output = (pre * sig).astype(jnp.bfloat16)
    dpre = (out_grad.astype(jnp.float32) * sig * (1.0 + pre * (1.0 - sig))).astype(jnp.bfloat16)
    total_nodes = nodes * parts * lax.axis_size("grp")
    scale = 1.0 / math.sqrt(total_nodes)
    contract = (((0,), (0,)), ((), ()))
    grad_self = lax.dot_general(features, dpre, contract, preferred_element_type=jnp.float32)
    grad_neigh = lax.dot_general(agg_low, dpre, contract, preferred_element_type=jnp.float32)
    agg_grad = jnp.dot(dpre, w_neigh.T, preferred_element_type=jnp.float32).astype(jnp.bfloat16)
    everyone = lax.all_gather(agg_grad, "dom", axis=0, tiled=True).reshape(
        parts * n_tiles, tile, width
    )
    picked = everyone[peers * n_tiles + dst_tile]
    back = jnp.einsum("tij,tif->tjf", adjacency, picked, preferred_element_type=jnp.float32)
    spread = (
        jnp.zeros((n_tiles, tile, width), jnp.float32).at[src_tile].add(back).reshape(nodes, width)
    )
    feat_grad = (jnp.dot(dpre, w_self.T, preferred_element_type=jnp.float32) + spread).astype(
        jnp.bfloat16
    )
    total_self, total_neigh = lax.psum((grad_self, grad_neigh), ("dom", "grp"))
    weight_grads = jnp.stack([total_self * scale, total_neigh * scale])
    return (output, feat_grad, weight_grads)


def solution(mesh):
    in_specs = (
        P(("dom", "grp"), None),
        P(("dom", "grp"), None, None),
        P(("dom", "grp")),
        P(("dom", "grp"), None),
        P(("dom", "grp")),
        P(),
        P(),
        P(("dom", "grp"), None),
    )
    out_specs = (P(("dom", "grp"), None), P(("dom", "grp"), None), P())
    return jax.shard_map(body, mesh=mesh, in_specs=in_specs, out_specs=out_specs, check_vma=False)
```

profile of v0, /device:TPU:1, one launch (start us, length us, event | category | flops | bytes accessed | tf_op | source)
XLA Modules:
  0.0 199.1 jit_solution(6476534840510673220)
XLA Ops:
  7.2 0.0 reduce-scatter.2.cloned.1.call-start
  7.2 0.7 compare_select_fusion
  7.9 2.5 %gather_fusion = bf16[16,128,256]{2,1,0:T(8,128)(2,1)} fusion(bf16[2,128,256]{2,1,0:T(8,128)(2,1)} %bitcast.34, s32[1024]{0:T(1024)S(1)} %pad_clamp_fusion.1), kind=kCustom, calls=%fused_computation | custom fusion | bytes 2097216 | tf_op jit(solution)/shard_map/gather | solution.py:16
  10.4 1.7 convert_bitcast_fusion
  12.2 1.9 copy.16
  14.0 0.1 broadcast_in_dim.14
  14.2 3.5 %scatter_fusion = f32[8,128,256]{2,1,0:T(8,128)S(1)} fusion(f32[8,128,256]{2,1,0:T(8,128)S(1)} %broadcast_in_dim.14, s32[16]{0:T(128)S(1)} %compare_select_fusion.1, f32[16,128,256]{2,1,0:T(8,128)} %copy.16), kind=kCustom, calls=%fused_computation.2 | custom fusion | flops 524288 | bytes 6291520 | tf_op jit(solution)/shard_map/scatter-add | solution.py:23
  17.7 1.0 copy-done.1
  18.7 0.0 all-reduce.3.cloned.1.call-start
  18.8 0.2 fusion.4
  19.0 29.7 %reduce-scatter.2.cloned.1.call-done = f32[256,256]{1,0:T(8,128)} async-done(((f32[1024,256]{1,0:T(8,128)}), f32[256,256]{1,0:T(8,128)}) %reduce-scatter.2.cloned.1.call-update) | async-done | bytes 262160 | tf_op jit(solution)/shard_map/reduce_scatter | solution.py:26
  48.6 2.0 multiply_convert_fusion
  50.6 0.9 convolution_bitcast_fusion.1
  51.5 0.2 convolution_convert_fusion.1
  51.7 7.9 %all_gather.3 = bf16[1024,256]{1,0:T(8,128)(2,1)S(1)} all-gather(bf16[256,256]{1,0:T(8,128)(2,1)S(1)} %convolution_convert_fusion.1), channel_id=1, replica_groups=mesh['dom'=4,'grp'=8] {'dom'}, dimensions={0}, use_global_device_ids=true | all-gather | bytes 655360 | tf_op jit(solution)/shard_map/all_gather | solution.py:40
  59.7 0.9 fusion.1
  60.7 0.6 gather_fusion.1
  61.3 1.8 convolution_bitcast_fusion
  63.1 1.9 copy.18
  65.1 2.2 %scatter_fusion.1 = f32[2,128,256]{2,1,0:T(8,128)S(1)} fusion(f32[2,128,256]{2,1,0:T(8,128)S(1)} %broadcast_in_dim.17, s32[16]{0:T(128)S(1)} %compare_select_fusion, f32[16,128,256]{2,1,0:T(8,128)S(1)} %copy.18), kind=kCustom, calls=%fused_computation.3 | custom fusion | flops 524288 | bytes 6291520 | tf_op jit(solution)/shard_map/scatter-add | solution.py:46
  67.2 0.9 fusion
  68.1 122.0 %all-reduce.3.cloned.1.call-done = (f32[256,256]{0,1:T(8,128)}, f32[256,256]{0,1:T(8,128)}) async-done(((f32[256,256]{0,1:T(8,128)}, f32[256,256]{0,1:T(8,128)}), (f32[256,256]{0,1:T(8,128)}, f32[256,256]{0,1:T(8,128)})) %all-reduce.3.cloned.1.call-update) | async-done | bytes 524304 | tf_op jit(solution)/shard_map/psum | solution.py:51
  190.1 1.1 multiply_bitcast_fusion
  191.2 1.0 copy.20
  (24 shorter events, 0.2 us)
Async XLA Ops:
  7.2 3.3 %copy-start = (bf16[16,128,128]{2,1,0:T(8,128)(2,1)S(1)}, bf16[16,128,128]{2,1,0:T(8,128)(2,1)}, u32[]{:S(2)}) copy-start(bf16[16,128,128]{2,1,0:T(8,128)(2,1)} %param.9) | copy-start | bytes 1572868
  7.2 41.5 %reduce-scatter.2.cloned.1.call-start = ((), (), s32[]{:S(2)}) async-start(), calls=%async_computation.1 | async-start | bytes 1310720 | tf_op jit(solution)/shard_map/reduce_scatter | solution.py:26
  12.1 1.9 copy-start.7
  12.1 1.9 copy-start.8
  14.1 4.6 %copy-start.2 = (bf16[256,256]{1,0:T(8,128)(2,1)S(1)}, bf16[256,256]{1,0:T(8,128)(2,1)}, u32[]{:S(2)}) copy-start(bf16[256,256]{1,0:T(8,128)(2,1)} %param.8) | copy-start | bytes 393220
  14.1 4.6 %copy-start.3 = (bf16[256,256]{1,0:T(8,128)(2,1)S(1)}, bf16[256,256]{1,0:T(8,128)(2,1)}, u32[]{:S(2)}) copy-start(bf16[256,256]{1,0:T(8,128)(2,1)} %param.13) | copy-start | bytes 393220
  14.2 34.5 %copy-start.5 = (bf16[256,256]{1,0:T(8,128)(2,1)S(1)}, bf16[256,256]{1,0:T(8,128)(2,1)}, u32[]{:S(2)}) copy-start(bf16[256,256]{1,0:T(8,128)(2,1)} %param.14) | copy-start | bytes 393220
  14.2 34.5 %copy-start.6 = (bf16[256,256]{1,0:T(8,128)(2,1)S(1)}, bf16[256,256]{1,0:T(8,128)(2,1)}, u32[]{:S(2)}) copy-start(bf16[256,256]{1,0:T(8,128)(2,1)} %param.15) | copy-start | bytes 393220
  17.7 1.0 copy-start.1
  18.7 171.4 %all-reduce.3.cloned.1.call-start = ((), (), s32[]{:S(2)}) async-start(), calls=%async_computation.2 | async-start | bytes 1048576 | tf_op jit(solution)/shard_map/psum | solution.py:51
  48.6 11.1 %copy-start.4 = (f32[256,256]{1,0:T(8,128)S(1)}, f32[256,256]{1,0:T(8,128)}, u32[]{:S(2)}) copy-start(f32[256,256]{1,0:T(8,128)} %reduce-scatter.2.cloned.1.call-done) | copy-start | bytes 786436
Sparse Core Ops, SparseCore 0:
  18.8 29.7 reduce-scatter.1
  60.8 129.2 all-reduce.2
where the time goes:
time: 201 us; the launch traced here: 199 us
  waiting for transfers between devices  152 us (76%)
  between operations  14.2 us (7%)
  local copies, waits for them, and re-layouts  9 us (4%)
  matrix products  8.63 us (4%)
  blocking collectives  7.95 us (4%)
  other arithmetic  7.51 us (4%)
    psum x1, waiting for transfers between devices, body(): total_self, total_neigh = lax.psum((grad_self, grad_neigh), ('dom', 'grp'))  122 us
    reduce_scatter x1, waiting for transfers between devices, body(): agg = lax.psum_scatter(flat, 'dom', scatter_dimension=0, tiled=True)  29.7 us
    all_gather x1, blocking collectives, body(): lax.all_gather(agg_grad, 'dom', axis=0, tiled=True)  7.95 us
  transfers between devices with their start and end apart: 2, of which 2 were waited for; matrix products, arithmetic and copies ran while one was open for 4% of the time, Pallas kernels for 0%

commit v1 on v0

v1 whole, which is shorter than its diff:
```python
import functools
import math

import jax
import jax.numpy as jnp
from jax import lax
from jax.experimental import pallas as pl
from jax.experimental.pallas import tpu as pltpu
from jax.sharding import PartitionSpec as P

MESH = pl.DeviceIdType.MESH
BF16 = jnp.bfloat16
F32 = jnp.float32
STRIP = 32
MIN_ROWS = 16
CORES = 2


def dot(a, b, ca=1, cb=0):
    return lax.dot_general(a, b, (((ca,), (cb,)), ((), ())), preferred_element_type=F32)


def kernel(
    parts, depth, reduce_here, scale,
    src_ref, peer_ref, tile_ref, x_ref, adj_ref, ws_ref, wn_ref, og_ref,
    out_ref, fg_ref, wg_ref,
    dense, fsend, frecv, gsend, grecv, both, wsend, wsib, wsum, wslots, wfull,
    fs_sem, fr_sem, gs_sem, gr_sem, sib_s, sib_r, rs_s, rs_r, ag_s, ag_r,
):
    dom = lax.axis_index("dom")
    grp = lax.axis_index("grp")
    count, tile = adj_ref.shape[0], adj_ref.shape[1]
    nodes, width = x_ref.shape
    nt = nodes // tile
    core = lax.rem(grp, CORES)
    layer = grp // CORES
    chips = parts * depth
    here = dom * depth + layer
    sibling = (dom, layer * CORES + (1 - core))

    def peer_at(k):
        return (lax.rem(dom + k, parts), grp)

    def chip_at(k):
        index = lax.rem(here + k, chips)
        return index, (index // depth, lax.rem(index, depth) * CORES + core)

    barrier = pltpu.get_barrier_semaphore()
    if reduce_here:
        for k in range(1, chips):
            pl.semaphore_signal(barrier, inc=1, device_id=chip_at(k)[1], device_id_type=MESH)
        pl.semaphore_signal(barrier, inc=1, device_id=sibling, device_id_type=MESH)
        greeted = chips
    else:
        for k in range(1, parts):
            pl.semaphore_signal(barrier, inc=1, device_id=peer_at(k), device_id_type=MESH)
        greeted = parts - 1

    codes = [(peer_ref[t] * nt + tile_ref[t]) * nt + src_ref[t] for t in range(count)]

    def build(k):
        base = lax.rem(dom + k, parts) * (nt * nt)
        marks = [
            [jnp.where(code - base == c, 1.0, 0.0).astype(F32) for c in range(nt * nt)]
            for code in codes
        ]

        def strip(i, carry):
            start = pl.multiple_of(i * STRIP, STRIP)
            sums = [jnp.zeros((STRIP, tile), F32) for _ in range(nt * nt)]
            for t in range(count):
                block = adj_ref[t, pl.ds(start, STRIP), :].astype(F32)
                for c in range(nt * nt):
                    sums[c] = sums[c] + marks[t][c] * block
            for c in range(nt * nt):
                rows = pl.ds((c // nt) * tile + start, STRIP)
                cols = pl.ds((c % nt) * tile, tile)
                dense[k, rows, cols] = sums[c].astype(BF16)
            return carry

        lax.fori_loop(0, tile // STRIP, strip, 0)

    def forward_copy(k):
        return pltpu.make_async_remote_copy(
            src_ref=fsend.at[k], dst_ref=frecv.at[k], send_sem=fs_sem.at[k], recv_sem=fr_sem.at[k],
            device_id=peer_at(k), device_id_type=MESH,
        )

    def gather_copy(k):
        return pltpu.make_async_remote_copy(
            src_ref=gsend, dst_ref=grecv.at[k], send_sem=gs_sem.at[k], recv_sem=gr_sem.at[k],
            device_id=peer_at(k), device_id_type=MESH,
        )

    x = x_ref[...]
    for k in range(1, parts):
        build(k)
        fsend[k] = dot(dense[k], x).astype(BF16)
        if k == 1:
            pl.semaphore_wait(barrier, greeted)
        forward_copy(k).start()
    build(0)
    agg = dot(dense[0], x)
    pre_self = dot(x, ws_ref[...])
    both[0] = x
    for k in range(1, parts):
        forward_copy(k).wait_recv()
        agg = agg + frecv[k].astype(F32)
    agg_low = agg.astype(BF16)
    both[1] = agg_low
    pre = pre_self + dot(agg_low, wn_ref[...])
    sig = jax.nn.sigmoid(pre)
    dpre = (og_ref[...].astype(F32) * sig * (1.0 + pre * (1.0 - sig))).astype(BF16)

    def sibling_copy(i, src, dst):
        return pltpu.make_async_remote_copy(
            src_ref=src, dst_ref=dst, send_sem=sib_s.at[i], recv_sem=sib_r.at[i],
            device_id=sibling, device_id_type=MESH,
        )

    if reduce_here:
        halving = sibling_copy(0, wsend, wsib)
        wsend[...] = dot(both[1 - core], dpre, 0, 0).astype(BF16)
        halving.start()
    gsend[...] = dot(dpre, wn_ref[...], 1, 1).astype(BF16)
    for k in range(1, parts):
        gather_copy(k).start()
    out_ref[...] = (pre * sig).astype(BF16)

    if reduce_here:
        rows = width // chips

        def scatter_copy(k):
            index, target = chip_at(k)
            start = pl.multiple_of(index * rows, rows)
            return pltpu.make_async_remote_copy(
                src_ref=wsum.at[pl.ds(start, rows)], dst_ref=wslots.at[k],
                send_sem=rs_s.at[k], recv_sem=rs_r.at[k], device_id=target, device_id_type=MESH,
            )

        mine = pl.ds(pl.multiple_of(here * rows, rows), rows)

        def spread_copy(k):
            return pltpu.make_async_remote_copy(
                src_ref=wfull.at[core, mine], dst_ref=wfull.at[core, mine],
                send_sem=ag_s.at[k], recv_sem=ag_r.at[k], device_id=chip_at(k)[1], device_id_type=MESH,
            )

        own = dot(both[core], dpre, 0, 0)
        halving.wait_recv()
        wsum[...] = (own + wsib[...].astype(F32)).astype(BF16)
        for k in range(1, chips):
            scatter_copy(k).start()
    else:
        wg_ref[0] = dot(x, dpre, 0, 0)
        wg_ref[1] = dot(agg_low, dpre, 0, 0)

    grad = dot(dpre, ws_ref[...], 1, 1) + dot(dense[0], gsend[...], 0, 0)

    if reduce_here:
        total = wsum[mine, :].astype(F32)
        for k in range(1, chips):
            scatter_copy(k).wait_recv()
            total = total + wslots[k].astype(F32)
        wfull[core, mine, :] = (total * scale).astype(BF16)
        for k in range(1, chips):
            spread_copy(k).start()

    for k in range(1, parts):
        gather_copy(k).wait_recv()
        grad = grad + dot(dense[parts - k], grecv[k], 0, 0)
    fg_ref[...] = grad.astype(BF16)

    if reduce_here:
        for k in range(1, chips):
            spread_copy(k).wait_recv()
        final = sibling_copy(1, wfull.at[core], wfull.at[core])
        final.start()
        wg_ref[core] = wfull[core]
        final.wait_recv()
        wg_ref[1 - core] = wfull[1 - core]
        halving.wait_send()
        final.wait_send()
        for k in range(1, chips):
            scatter_copy(k).wait_send()
            spread_copy(k).wait_send()
    for k in range(1, parts):
        forward_copy(k).wait_send()
        gather_copy(k).wait_send()


def body(features, adjacency, src_tile, dst_peer, dst_tile, w_self, w_neigh, out_grad):
    nodes, width = features.shape
    parts, groups = lax.axis_size("dom"), lax.axis_size("grp")
    depth = groups // CORES
    chips = parts * depth
    reduce_here = width % chips == 0 and (width // chips) % MIN_ROWS == 0
    scale = 1.0 / math.sqrt(nodes * parts * groups)
    rows = width // chips if reduce_here else MIN_ROWS
    slots = chips if reduce_here else 1
    vmem = pl.BlockSpec(memory_space=pltpu.VMEM)
    smem = pl.BlockSpec(memory_space=pltpu.SMEM)
    square = (nodes, width)
    dma = pltpu.SemaphoreType.DMA
    output, feat_grad, grads = pl.pallas_call(
        functools.partial(kernel, parts, depth, reduce_here, scale),
        out_shape=(
            jax.ShapeDtypeStruct(square, BF16),
            jax.ShapeDtypeStruct(square, BF16),
            jax.ShapeDtypeStruct((2, width, width), BF16 if reduce_here else F32),
        ),
        in_specs=[smem] * 3 + [vmem] * 5,
        out_specs=(vmem, vmem, vmem),
        scratch_shapes=[
            pltpu.VMEM((parts, nodes, nodes), BF16),
            pltpu.VMEM((parts,) + square, BF16),
            pltpu.VMEM((parts,) + square, BF16),
            pltpu.VMEM(square, BF16),
            pltpu.VMEM((parts,) + square, BF16),
            pltpu.VMEM((2,) + square, BF16),
            pltpu.VMEM((width, width), BF16),
            pltpu.VMEM((width, width), BF16),
            pltpu.VMEM((width, width), BF16),
            pltpu.VMEM((slots, rows, width), BF16),
            pltpu.VMEM((2, width, width), BF16),
            dma((parts,)), dma((parts,)), dma((parts,)), dma((parts,)),
            dma((2,)), dma((2,)),
            dma((slots,)), dma((slots,)), dma((slots,)), dma((slots,)),
        ],
        compiler_params=pltpu.CompilerParams(
            collective_id=0, has_side_effects=True, vmem_limit_bytes=48 * 1024 * 1024
        ),
        name="sage_layer",
    )(src_tile, dst_peer[:, 0], dst_tile, features, adjacency, w_self, w_neigh, out_grad)
    if reduce_here:
        weight_grads = grads.astype(F32)
    else:
        weight_grads = lax.psum(grads, ("dom", "grp")) * scale
    return (output, feat_grad, weight_grads)


def solution(mesh):
    shard = ("dom", "grp")
    in_specs = (
        P(shard, None),
        P(shard, None, None),
        P(shard),
        P(shard, None),
        P(shard),
        P(),
        P(),
        P(shard, None),
    )
    out_specs = (P(shard, None), P(shard, None), P())
    return jax.shard_map(body, mesh=mesh, in_specs=in_specs, out_specs=out_specs, check_vma=False)
```

time: 201 us -> 38.9 us (0.19)
  waiting for transfers between devices: 152 us -> 0 us
  Pallas kernels: 0 us -> 30.5 us
  between operations: 14.2 us -> 0.67 us
  matrix products: 8.63 us -> 0 us
  blocking collectives: 7.95 us -> 0 us
  other arithmetic: 7.51 us -> 0.83 us
  local copies, waits for them, and re-layouts: 9 us -> 6.63 us
    psum x1 -> x0, waiting for transfers between devices: 122 us -> none  [body(): total_self, total_neigh = lax.psum((grad_self, grad_neigh), ('dom', 'grp'))]
    pallas_call x0 -> x1, Pallas kernels: none -> 30.5 us  [body(): pl.pallas_call(functools.partial(kernel, parts, depth, reduce_here, scale...]
    reduce_scatter x1 -> x0, waiting for transfers between devices: 29.7 us -> none  [body(): agg = lax.psum_scatter(flat, 'dom', scatter_dimension=0, tiled=True)]
    dot_general x8 -> x0, matrix products: 8.63 us -> none  [the longest x1 1.96 us: body(): jnp.dot(agg_low, w_neigh, preferred_element_type=jnp.float32)]
    all_gather x1 -> x0, blocking collectives: 7.95 us -> none  [body(): lax.all_gather(agg_grad, 'dom', axis=0, tiled=True)]
    scatter-add x2 -> x0, other arithmetic: 5.67 us -> none  [the longest x1 3.5 us: body(): dense = jnp.zeros((parts * n_tiles, tile, width), jnp.float32).at[target]...]
    unnamed x19 -> x18, local copies, waits for them, and re-layouts: 2.01 us -> 6.63 us
    gather x2 -> x0, local copies, waits for them, and re-layouts: 3.1 us -> none  [the longest x1 2.48 us: body(): blocks[src_tile]]
  transfers between devices with their start and end apart: 2 -> 0, of which waited for: 2 -> 0; matrix products, arithmetic and copies ran while one was open for 4% -> 0% of each run, Pallas kernels for 0% -> 0%
where the time goes in v1:
time: 38.9 us; the launch traced here: 38.6 us
  Pallas kernels  30.5 us (78%)
  local copies, waits for them, and re-layouts  6.63 us (17%)
  other arithmetic  0.83 us (2%)
  between operations  0.67 us (2%)
    pallas_call x1, Pallas kernels, body(): pl.pallas_call(functools.partial(kernel, parts, depth, reduce_here, scale...  30.5 us
    unnamed x18, local copies, waits for them, and re-layouts  6.63 us
    convert_element_type x1, other arithmetic, body(): weight_grads = grads.astype(F32)  0.83 us

profile of v1, /device:TPU:1, one launch (start us, length us, event | category | flops | bytes accessed | tf_op | source)
XLA Modules:
  0.0 38.6 jit_solution(15888012738984862437)
XLA Ops:
  0.6 0.0 copy-start.7
  0.6 0.0 copy-start.6
  0.7 0.0 copy-start.5
  0.7 0.6 %copy-done.7 = s32[16]{0:T(128)S(1)} copy-done((s32[16]{0:T(128)S(1)}, s32[16]{0:T(128)}, u32[]{:S(2)}) %copy-start.7) | copy-done | bytes 88
  1.3 0.0 copy-done.6
  1.3 0.0 copy-done.5
  1.3 0.0 copy-start
  1.3 1.0 %copy-done = bf16[16,128,128]{2,1,0:T(8,128)(2,1)S(1)} copy-done((bf16[16,128,128]{2,1,0:T(8,128)(2,1)S(1)}, bf16[16,128,128]{2,1,0:T(8,128)(2,1)}, u32[]{:S(2)}) %copy-start) | copy-done | bytes 524312
  2.4 0.0 copy-start.1
  2.4 0.9 %copy-done.1 = bf16[256,256]{1,0:T(8,128)(2,1)S(1)} copy-done((bf16[256,256]{1,0:T(8,128)(2,1)S(1)}, bf16[256,256]{1,0:T(8,128)(2,1)}, u32[]{:S(2)}) %copy-start.1) | copy-done | bytes 131096
  3.3 0.0 copy-start.2
  3.3 0.9 %copy-done.2 = bf16[256,256]{1,0:T(8,128)(2,1)S(1)} copy-done((bf16[256,256]{1,0:T(8,128)(2,1)S(1)}, bf16[256,256]{1,0:T(8,128)(2,1)}, u32[]{:S(2)}) %copy-start.2) | copy-done | bytes 131096
  4.2 0.0 copy-start.3
  4.2 0.9 %copy-done.3 = bf16[256,256]{1,0:T(8,128)(2,1)S(1)} copy-done((bf16[256,256]{1,0:T(8,128)(2,1)S(1)}, bf16[256,256]{1,0:T(8,128)(2,1)}, u32[]{:S(2)}) %copy-start.3) | copy-done | bytes 131096
  5.1 0.0 copy-start.4
  5.1 0.9 %copy-done.4 = bf16[256,256]{1,0:T(8,128)(2,1)S(1)} copy-done((bf16[256,256]{1,0:T(8,128)(2,1)S(1)}, bf16[256,256]{1,0:T(8,128)(2,1)}, u32[]{:S(2)}) %copy-start.4) | copy-done | bytes 131096
  6.0 30.5 %sage_layer.1 = (bf16[256,256]{1,0:T(8,128)(2,1)S(1)}, bf16[256,256]{1,0:T(8,128)(2,1)S(1)}, bf16[2,256,256]{2,1,0:T(8,128)(2,1)S(1)}) custom-call(s32[16]{0:T(128)S(1)} %copy-done.5, s32[16]{0:T(128)S(1)} %bitcast.1, s32[16]{0:T(128)S(1)} %copy-done.7, bf16[256,256]{1,0:T(8,128)(2,1)S(1)} %copy-done.1, bf16[16,128,128]{2,1,0:T(8,128)(2,1)S(1)} %copy-done, ...), custom_call_target="tpu_custom_call" | custom-call | tf_op jit(solution)/shard_map/sage_layer/pallas_call | solution.py:205
  36.4 0.8 %convert_element_type.3 = f32[2,256,256]{2,1,0:T(8,128)} convert(bf16[2,256,256]{2,1,0:T(8,128)(2,1)S(1)} %get-tuple-element.8) | non-fusion elementwise | flops 131072 | bytes 786432 | tf_op jit(solution)/shard_map/convert_element_type | solution.py:236
  37.3 0.7 %copy.13 = bf16[256,256]{1,0:T(8,128)(2,1)} copy(bf16[256,256]{1,0:T(8,128)(2,1)S(1)} %get-tuple-element.12) | data formatting | bytes 262144
  37.9 0.7 %copy.14 = bf16[256,256]{1,0:T(8,128)(2,1)} copy(bf16[256,256]{1,0:T(8,128)(2,1)S(1)} %get-tuple-element.13) | data formatting | bytes 262144
Async XLA Ops:
  0.6 0.7 %copy-start.7 = (s32[16]{0:T(128)S(1)}, s32[16]{0:T(128)}, u32[]{:S(2)}) copy-start(s32[16]{0:T(128)} %tile_ref.1) | copy-start | bytes 196
  0.6 0.7 %copy-start.6 = (s32[16,1]{0,1:T(1,128)S(1)}, s32[16,1]{0,1:T(1,128)}, u32[]{:S(2)}) copy-start(s32[16,1]{0,1:T(1,128)} %param.11) | copy-start | bytes 196
  0.7 0.7 %copy-start.5 = (s32[16]{0:T(128)S(1)}, s32[16]{0:T(128)}, u32[]{:S(2)}) copy-start(s32[16]{0:T(128)} %src_ref.1) | copy-start | bytes 196
  1.3 1.0 %copy-start = (bf16[16,128,128]{2,1,0:T(8,128)(2,1)S(1)}, bf16[16,128,128]{2,1,0:T(8,128)(2,1)}, u32[]{:S(2)}) copy-start(bf16[16,128,128]{2,1,0:T(8,128)(2,1)} %adj_ref.1) | copy-start | bytes 1572868
  2.4 0.9 %copy-start.1 = (bf16[256,256]{1,0:T(8,128)(2,1)S(1)}, bf16[256,256]{1,0:T(8,128)(2,1)}, u32[]{:S(2)}) copy-start(bf16[256,256]{1,0:T(8,128)(2,1)} %x_ref.1) | copy-start | bytes 393220
  3.3 0.9 %copy-start.2 = (bf16[256,256]{1,0:T(8,128)(2,1)S(1)}, bf16[256,256]{1,0:T(8,128)(2,1)}, u32[]{:S(2)}) copy-start(bf16[256,256]{1,0:T(8,128)(2,1)} %ws_ref.1) | copy-start | bytes 393220
  4.2 0.9 %copy-start.3 = (bf16[256,256]{1,0:T(8,128)(2,1)S(1)}, bf16[256,256]{1,0:T(8,128)(2,1)}, u32[]{:S(2)}) copy-start(bf16[256,256]{1,0:T(8,128)(2,1)} %wn_ref.1) | copy-start | bytes 393220
  5.1 0.9 %copy-start.4 = (bf16[256,256]{1,0:T(8,128)(2,1)S(1)}, bf16[256,256]{1,0:T(8,128)(2,1)}, u32[]{:S(2)}) copy-start(bf16[256,256]{1,0:T(8,128)(2,1)} %og_ref.1) | copy-start | bytes 393220

commit v2 on v1

v2 whole, which is shorter than its diff:
```python
import functools
import math

import jax
import jax.numpy as jnp
from jax import lax
from jax.experimental import pallas as pl
from jax.experimental.pallas import tpu as pltpu
from jax.sharding import PartitionSpec as P

MESH = pl.DeviceIdType.MESH
BF16 = jnp.bfloat16
F32 = jnp.float32
STRIP = 32
MIN_ROWS = 16
CORES = 2
GROUP = 4
VMEM_BYTES = 63 * 1024 * 1024


def dot(a, b, ca=1, cb=0):
    return lax.dot_general(a, b, (((ca,), (cb,)), ((), ())), preferred_element_type=F32)


def flip(index, k, size):
    total, bit = 0, 1
    while bit < size:
        digit = lax.rem(index // bit, 2)
        total = total + bit * ((1 - digit) if (k // bit) % 2 else digit)
        bit *= 2
    return total


def kernel(
    parts, depth, reduce_here, scale,
    src_hbm, peer_hbm, tile_hbm, x_hbm, adj_hbm, ws_hbm, wn_hbm, og_hbm,
    out_hbm, fg_hbm, wg_hbm,
    src_ref, peer_ref, tile_ref, x_ref, adj_ref, ws_ref, wn_ref, og_ref,
    dense, dense_t, fsend, frecv, gsend, grecv, both_t, wsend, wsib, wsum, wslots, wfull, out_ref, fg_ref, wg_ref,
    in_sem, out_sem, fs_sem, fr_sem, gs_sem, gr_sem, sib_s, sib_r, rs_s, rs_r, ag_s, ag_r,
):
    dom = lax.axis_index("dom")
    grp = lax.axis_index("grp")
    count, tile = adj_ref.shape[0], adj_ref.shape[1]
    nodes, width = x_ref.shape
    nt = nodes // tile
    core = lax.rem(grp, CORES)
    layer = grp // CORES
    chips = parts * depth
    here = dom * depth + layer
    sibling = (dom, layer * CORES + (1 - core))

    loads = [
        pltpu.make_async_copy(hbm, local, in_sem.at[i])
        for i, (hbm, local) in enumerate([
            (peer_hbm, peer_ref), (tile_hbm, tile_ref), (src_hbm, src_ref), (adj_hbm, adj_ref),
            (x_hbm, x_ref), (ws_hbm, ws_ref), (wn_hbm, wn_ref), (og_hbm, og_ref),
        ])
    ]
    for load in loads:
        load.start()

    peers = [flip(dom, k, parts) for k in range(parts)]

    def chip_at(k):
        index = flip(here, k, chips)
        return index, (index // depth, lax.rem(index, depth) * CORES + core)

    barrier = pltpu.get_barrier_semaphore()
    if reduce_here:
        chip_ids = [chip_at(k) for k in range(chips)]
        for k in range(1, chips):
            pl.semaphore_signal(barrier, inc=1, device_id=chip_ids[k][1], device_id_type=MESH)
        pl.semaphore_signal(barrier, inc=1, device_id=sibling, device_id_type=MESH)
        greeted = chips
    else:
        for k in range(1, parts):
            pl.semaphore_signal(barrier, inc=1, device_id=(peers[k], grp), device_id_type=MESH)
        greeted = parts - 1

    for load in loads[:5]:
        load.wait()
    codes = [(peer_ref[t] * nt + tile_ref[t]) * nt + src_ref[t] for t in range(count)]

    def build(k):
        base = peers[k] * (nt * nt)
        marks = [
            [jnp.where(code - base == c, 1.0, 0.0).astype(F32) for c in range(nt * nt)]
            for code in codes
        ]

        def strip(i, carry):
            start = pl.multiple_of(i * STRIP, STRIP)
            sums = [jnp.zeros((STRIP, tile), F32) for _ in range(nt * nt)]
            for t in range(count):
                block = adj_ref[t, pl.ds(start, STRIP), :].astype(F32)
                for c in range(nt * nt):
                    sums[c] = sums[c] + marks[t][c] * block
            for c in range(nt * nt):
                rows = pl.ds((c // nt) * tile + start, STRIP)
                cols = pl.ds((c % nt) * tile, tile)
                dense[k, rows, cols] = sums[c].astype(BF16)
            return carry

        lax.fori_loop(0, tile // STRIP, strip, 0)

    def forward_copy(k):
        return pltpu.make_async_remote_copy(
            src_ref=fsend.at[k], dst_ref=frecv.at[k], send_sem=fs_sem.at[k], recv_sem=fr_sem.at[k],
            device_id=(peers[k], grp), device_id_type=MESH,
        )

    def gather_copy(k):
        return pltpu.make_async_remote_copy(
            src_ref=gsend, dst_ref=grecv.at[k], send_sem=gs_sem.at[k], recv_sem=gr_sem.at[k],
            device_id=(peers[k], grp), device_id_type=MESH,
        )

    x = x_ref[...]
    order = list(range(parts - 1, 0, -1))
    for k in order:
        build(k)
        fsend[k] = dot(dense[k], x).astype(BF16)
        if k == order[0]:
            pl.semaphore_wait(barrier, greeted)
        forward_copy(k).start()
    build(0)
    for load in loads[5:]:
        load.wait()
    agg = dot(dense[0], x)
    pre_self = dot(x, ws_ref[...])
    both_t[0] = x.T
    for k in range(parts):
        dense_t[k] = dense[k].T
    for k in order:
        forward_copy(k).wait_recv()
        agg = agg + frecv[k].astype(F32)
    agg_low = agg.astype(BF16)
    both_t[1] = agg_low.T
    pre = pre_self + dot(agg_low, wn_ref[...])
    sig = jax.nn.sigmoid(pre)
    dpre = (og_ref[...].astype(F32) * sig * (1.0 + pre * (1.0 - sig))).astype(BF16)

    def sibling_copy(i, src, dst):
        return pltpu.make_async_remote_copy(
            src_ref=src, dst_ref=dst, send_sem=sib_s.at[i], recv_sem=sib_r.at[i],
            device_id=sibling, device_id_type=MESH,
        )

    if reduce_here:
        halving = sibling_copy(chips // GROUP, wsend, wsib)
        wsend[...] = dot(both_t[1 - core], dpre).astype(BF16)
        halving.start()
    gsend[...] = dot(dpre, wn_ref[...], 1, 1).astype(BF16)
    for k in order:
        gather_copy(k).start()

    if reduce_here:
        rows = width // chips

        def scatter_copy(k):
            index, target = chip_ids[k]
            start = pl.multiple_of(index * rows, rows)
            return pltpu.make_async_remote_copy(
                src_ref=wsum.at[pl.ds(start, rows)], dst_ref=wslots.at[k],
                send_sem=rs_s.at[k], recv_sem=rs_r.at[k], device_id=target, device_id_type=MESH,
            )

        mine = pl.ds(pl.multiple_of(here * rows, rows), rows)

        def spread_copy(k):
            return pltpu.make_async_remote_copy(
                src_ref=wfull.at[core, mine], dst_ref=wfull.at[core, mine],
                send_sem=ag_s.at[k], recv_sem=ag_r.at[k], device_id=chip_ids[k][1], device_id_type=MESH,
            )

        own = dot(both_t[core], dpre)
        halving.wait_recv()
        wsum[...] = (own + wsib[...].astype(F32)).astype(BF16)
        for k in range(chips - 1, 0, -1):
            scatter_copy(k).start()
    else:
        wg_ref[0] = dot(both_t[0], dpre)
        wg_ref[1] = dot(both_t[1], dpre)
        whole = pltpu.make_async_copy(wg_ref, wg_hbm, out_sem.at[2])
        whole.start()

    out_ref[...] = (pre * sig).astype(BF16)
    stores = [
        pltpu.make_async_copy(out_ref, out_hbm, out_sem.at[0]),
        pltpu.make_async_copy(fg_ref, fg_hbm, out_sem.at[1]),
    ]
    stores[0].start()
    grad = dot(dpre, ws_ref[...], 1, 1) + dot(dense_t[0], gsend[...])

    if reduce_here:
        total = wsum[mine, :].astype(F32)
        for k in range(1, chips):
            scatter_copy(k).wait_recv()
            total = total + wslots[k].astype(F32)
        wfull[core, mine, :] = (total * scale).astype(BF16)
        for k in range(chips - 1, 0, -1):
            spread_copy(k).start()

    for k in order[::-1]:
        gather_copy(k).wait_recv()
        grad = grad + dot(dense_t[k], grecv[k])
    fg_ref[...] = grad.astype(BF16)
    stores[1].start()

    if reduce_here:
        finals = []
        for j in range(chips // GROUP):
            for k in range(j * GROUP, j * GROUP + GROUP):
                if k:
                    spread_copy(k).wait_recv()
            first = flip(here // GROUP, j, chips // GROUP) * (GROUP * rows)
            piece = wfull.at[core, pl.ds(pl.multiple_of(first, GROUP * rows), GROUP * rows)]
            finals.append(sibling_copy(j, piece, piece))
            finals[-1].start()
        first_half = pltpu.make_async_copy(wg_ref.at[core], wg_hbm.at[core], out_sem.at[2])
        other_half = pltpu.make_async_copy(wg_ref.at[1 - core], wg_hbm.at[1 - core], out_sem.at[3])
        wg_ref[core] = wfull[core].astype(F32)
        first_half.start()
        for final in finals:
            final.wait_recv()
        wg_ref[1 - core] = wfull[1 - core].astype(F32)
        other_half.start()
        stores += [first_half, other_half]
        halving.wait_send()
        for final in finals:
            final.wait_send()
        for k in range(1, chips):
            scatter_copy(k).wait_send()
            spread_copy(k).wait_send()
    else:
        stores.append(whole)
    for k in order:
        forward_copy(k).wait_send()
        gather_copy(k).wait_send()
    for store in stores:
        store.wait()


def finish(out_ref, fg_ref, wg_ref, out_hbm, fg_hbm, wg_hbm, sem):
    copies = [
        pltpu.make_async_copy(wg_ref.at[0], wg_hbm.at[0], sem.at[0]),
        pltpu.make_async_copy(wg_ref.at[1], wg_hbm.at[1], sem.at[1]),
        pltpu.make_async_copy(out_ref, out_hbm, sem.at[2]),
        pltpu.make_async_copy(fg_ref, fg_hbm, sem.at[3]),
    ]
    for copy in copies:
        copy.start()
    for copy in copies:
        copy.wait()


def body(features, adjacency, src_tile, dst_peer, dst_tile, w_self, w_neigh, out_grad):
    nodes, width = features.shape
    parts, groups = lax.axis_size("dom"), lax.axis_size("grp")
    depth = groups // CORES
    chips = parts * depth
    reduce_here = width % chips == 0 and (width // chips) % MIN_ROWS == 0
    scale = 1.0 / math.sqrt(nodes * parts * groups)
    rows = width // chips if reduce_here else MIN_ROWS
    slots = chips if reduce_here else 1
    hbm = pl.BlockSpec(memory_space=pltpu.HBM)
    square = (nodes, width)
    dma = pltpu.SemaphoreType.DMA
    output, feat_grad, grads = pl.pallas_call(
        functools.partial(kernel, parts, depth, reduce_here, scale),
        out_shape=(
            jax.ShapeDtypeStruct(square, BF16),
            jax.ShapeDtypeStruct(square, BF16),
            jax.ShapeDtypeStruct((2, width, width), F32),
        ),
        in_specs=[hbm] * 8,
        out_specs=(hbm, hbm, hbm),
        scratch_shapes=[
            pltpu.SMEM(src_tile.shape, jnp.int32),
            pltpu.SMEM(src_tile.shape, jnp.int32),
            pltpu.SMEM(src_tile.shape, jnp.int32),
            pltpu.VMEM(square, BF16),
            pltpu.VMEM(adjacency.shape, BF16),
            pltpu.VMEM(w_self.shape, BF16),
            pltpu.VMEM(w_neigh.shape, BF16),
            pltpu.VMEM(square, BF16),
            pltpu.VMEM((parts, nodes, nodes), BF16),
            pltpu.VMEM((parts, nodes, nodes), BF16),
            pltpu.VMEM((parts,) + square, BF16),
            pltpu.VMEM((parts,) + square, BF16),
            pltpu.VMEM(square, BF16),
            pltpu.VMEM((parts,) + square, BF16),
            pltpu.VMEM((2, width, nodes), BF16),
            pltpu.VMEM((width, width), BF16),
            pltpu.VMEM((width, width), BF16),
            pltpu.VMEM((width, width), BF16),
            pltpu.VMEM((slots, rows, width), BF16),
            pltpu.VMEM((2, width, width), BF16),
            pltpu.VMEM(square, BF16),
            pltpu.VMEM(square, BF16),
            pltpu.VMEM((2, width, width), F32),
            dma((8,)), dma((4,)), dma((parts,)), dma((parts,)), dma((parts,)), dma((parts,)),
            dma((chips // GROUP + 1,)), dma((chips // GROUP + 1,)),
            dma((slots,)), dma((slots,)), dma((slots,)), dma((slots,)),
        ],
        compiler_params=pltpu.CompilerParams(
            collective_id=0, has_side_effects=True, vmem_limit_bytes=VMEM_BYTES
        ),
        name="sage_layer",
    )(src_tile, dst_peer[:, 0], dst_tile, features, adjacency, w_self, w_neigh, out_grad)
    if not reduce_here:
        return (output, feat_grad, lax.psum(grads, ("dom", "grp")) * scale)
    return pl.pallas_call(
        finish,
        out_shape=(
            jax.ShapeDtypeStruct(square, BF16),
            jax.ShapeDtypeStruct(square, BF16),
            jax.ShapeDtypeStruct((2, width, width), F32),
        ),
        in_specs=[hbm] * 3,
        out_specs=(hbm, hbm, hbm),
        scratch_shapes=[dma((4,))],
        compiler_params=pltpu.CompilerParams(vmem_limit_bytes=VMEM_BYTES),
        name="write_results",
    )(output, feat_grad, grads)


def solution(mesh):
    shard = ("dom", "grp")
    in_specs = (
        P(shard, None),
        P(shard, None, None),
        P(shard),
        P(shard, None),
        P(shard),
        P(),
        P(),
        P(shard, None),
    )
    out_specs = (P(shard, None), P(shard, None), P())
    return jax.shard_map(body, mesh=mesh, in_specs=in_specs, out_specs=out_specs, check_vma=False)
```

time: 38.9 us -> 56.3 us (1.45)
  Pallas kernels: 30.5 us -> 55.5 us
  local copies, waits for them, and re-layouts: 6.63 us -> 0 us
  other arithmetic: 0.83 us -> 0 us
    pallas_call x0 -> x1, Pallas kernels: none -> 25 us  [body(): pl.pallas_call(finish, out_shape=(jax.ShapeDtypeStruct(square, BF16), jax...]
    unnamed x18 -> x0, local copies, waits for them, and re-layouts: 6.63 us -> none
    convert_element_type x1 -> x0, other arithmetic: 0.83 us -> none  [body(): weight_grads = grads.astype(F32)]
where the time goes in v2:
time: 56.3 us; the launch traced here: 56.1 us
  Pallas kernels  55.5 us (99%)
  between operations  0.64 us (1%)
    pallas_call x1, Pallas kernels, body(): pl.pallas_call(functools.partial(kernel, parts, depth, reduce_here, scale...  30.5 us
    pallas_call x1, Pallas kernels, body(): pl.pallas_call(finish, out_shape=(jax.ShapeDtypeStruct(square, BF16), jax...  25 us

profile of v2, /device:TPU:1, one launch (start us, length us, event | category | flops | bytes accessed | tf_op | source)
XLA Modules:
  0.0 56.1 jit_solution(3121372118344391482)
XLA Ops:
  0.6 30.5 %sage_layer.1 = (bf16[256,256]{1,0:T(8,128)(2,1)}, bf16[256,256]{1,0:T(8,128)(2,1)}, f32[2,256,256]{2,1,0:T(8,128)}) custom-call(s32[16]{0:T(128)} %src_hbm.1, s32[16]{0:T(128)} %bitcast.1, s32[16]{0:T(128)} %tile_hbm.1, bf16[256,256]{1,0:T(8,128)(2,1)} %x_hbm.1, bf16[16,128,128]{2,1,0:T(8,128)(2,1)} %adj_hbm.1, bf16[256,256]{1,0:T(8,128)(2,1)} %ws_hbm.1, ...), custom_call_target="tpu_custom_call" | custom-call | tf_op jit(solution)/shard_map/sage_layer/pallas_call | solution.py:270
  31.2 25.0 %write_results.1 = (bf16[256,256]{1,0:T(8,128)(2,1)}, bf16[256,256]{1,0:T(8,128)(2,1)}, f32[2,256,256]{2,1,0:T(8,128)}) custom-call(bf16[256,256]{1,0:T(8,128)(2,1)} %get-tuple-element.6.out_ref, bf16[256,256]{1,0:T(8,128)(2,1)} %get-tuple-element.7.fg_ref, f32[2,256,256]{2,1,0:T(8,128)} %get-tuple-element.8.wg_ref), custom_call_target="tpu_custom_call" | custom-call | tf_op jit(solution)/shard_map/write_results/pallas_call | solution.py:314

commit v3 on v2

v3 whole, which is shorter than its diff:
```python
import functools
import math

import jax
import jax.numpy as jnp
from jax import lax
from jax.experimental import pallas as pl
from jax.experimental.pallas import tpu as pltpu
from jax.sharding import PartitionSpec as P

MESH = pl.DeviceIdType.MESH
BF16 = jnp.bfloat16
F32 = jnp.float32
STRIP = 32
CORES = 2
VMEM_BYTES = 63 * 1024 * 1024


def dot(a, b, ca=1, cb=0):
    return lax.dot_general(a, b, (((ca,), (cb,)), ((), ())), preferred_element_type=F32)


def flip(index, k, size):
    total, bit = 0, 1
    while bit < size:
        digit = lax.rem(index // bit, 2)
        total = total + bit * ((1 - digit) if (k // bit) % 2 else digit)
        bit *= 2
    return total


def kernel(
    parts, depth, scale,
    src_hbm, peer_hbm, tile_hbm, x_hbm, adj_hbm, ws_hbm, wn_hbm, og_hbm,
    out_hbm, fg_hbm, wg_hbm,
    src_ref, peer_ref, tile_ref, x_ref, adj_ref, ws_ref, wn_ref, og_ref,
    dense, dense_t, fsend, frecv, gsend, grecv, both_t, wsend, wsib, wsum, dslots, zslots, wfull, out_ref, fg_ref, wg_ref, local_sum,
    in_sem, out_sem, fs_sem, fr_sem, gs_sem, gr_sem, sib_s, sib_r, rs_s, rs_r, z_s, z_r, ag_s, ag_r,
):
    dom = lax.axis_index("dom")
    grp = lax.axis_index("grp")
    count, tile = adj_ref.shape[0], adj_ref.shape[1]
    nodes, width = x_ref.shape
    nt = nodes // tile
    core = lax.rem(grp, CORES)
    layer = grp // CORES
    rows = width // parts
    sibling = (dom, layer * CORES + (1 - core))

    loads = [
        pltpu.make_async_copy(hbm, local, in_sem.at[i])
        for i, (hbm, local) in enumerate([
            (peer_hbm, peer_ref), (tile_hbm, tile_ref), (src_hbm, src_ref), (adj_hbm, adj_ref),
            (x_hbm, x_ref), (ws_hbm, ws_ref), (wn_hbm, wn_ref), (og_hbm, og_ref),
        ])
    ]
    for load in loads:
        load.start()

    peers = [flip(dom, k, parts) for k in range(parts)]

    layers = [(dom, flip(layer, k, depth) * CORES + core) for k in range(depth)]

    barrier = pltpu.get_barrier_semaphore()
    partners = [(peers[k], grp) for k in range(1, parts)] + layers[1:] + [sibling]
    for partner in partners:
        pl.semaphore_signal(barrier, inc=1, device_id=partner, device_id_type=MESH)

    for load in loads[:5]:
        load.wait()
    codes = [(peer_ref[t] * nt + tile_ref[t]) * nt + src_ref[t] for t in range(count)]

    def build(k):
        base = peers[k] * (nt * nt)
        marks = [
            [jnp.where(code - base == c, 1.0, 0.0).astype(F32) for c in range(nt * nt)]
            for code in codes
        ]

        def strip(i, carry):
            start = pl.multiple_of(i * STRIP, STRIP)
            sums = [jnp.zeros((STRIP, tile), F32) for _ in range(nt * nt)]
            for t in range(count):
                block = adj_ref[t, pl.ds(start, STRIP), :].astype(F32)
                for c in range(nt * nt):
                    sums[c] = sums[c] + marks[t][c] * block
            for c in range(nt * nt):
                rows = pl.ds((c // nt) * tile + start, STRIP)
                cols = pl.ds((c % nt) * tile, tile)
                dense[k, rows, cols] = sums[c].astype(BF16)
            return carry

        lax.fori_loop(0, tile // STRIP, strip, 0)

    def forward_copy(k):
        return pltpu.make_async_remote_copy(
            src_ref=fsend.at[k], dst_ref=frecv.at[k], send_sem=fs_sem.at[k], recv_sem=fr_sem.at[k],
            device_id=(peers[k], grp), device_id_type=MESH,
        )

    def gather_copy(k):
        return pltpu.make_async_remote_copy(
            src_ref=gsend, dst_ref=grecv.at[k], send_sem=gs_sem.at[k], recv_sem=gr_sem.at[k],
            device_id=(peers[k], grp), device_id_type=MESH,
        )

    x = x_ref[...]
    order = list(range(parts - 1, 0, -1))
    for k in order:
        build(k)
        fsend[k] = dot(dense[k], x).astype(BF16)
        if k == order[0]:
            pl.semaphore_wait(barrier, len(partners))
        forward_copy(k).start()
    build(0)
    for load in loads[5:]:
        load.wait()
    agg = dot(dense[0], x)
    pre_self = dot(x, ws_ref[...])
    both_t[0] = x.T
    for k in range(parts):
        dense_t[k] = dense[k].T
    for k in order:
        forward_copy(k).wait_recv()
        agg = agg + frecv[k].astype(F32)
    agg_low = agg.astype(BF16)
    both_t[1] = agg_low.T
    pre = pre_self + dot(agg_low, wn_ref[...])
    sig = jax.nn.sigmoid(pre)
    dpre = (og_ref[...].astype(F32) * sig * (1.0 + pre * (1.0 - sig))).astype(BF16)

    def sibling_copy(i, src, dst):
        return pltpu.make_async_remote_copy(
            src_ref=src, dst_ref=dst, send_sem=sib_s.at[i], recv_sem=sib_r.at[i],
            device_id=sibling, device_id_type=MESH,
        )

    halving = sibling_copy(parts, wsend, wsib)
    wsend[...] = dot(both_t[1 - core], dpre).astype(BF16)
    halving.start()
    gsend[...] = dot(dpre, wn_ref[...], 1, 1).astype(BF16)
    own = dot(both_t[core], dpre)

    def scatter_copy(k):
        start = pl.multiple_of(peers[k] * rows, rows)
        return pltpu.make_async_remote_copy(
            src_ref=wsum.at[pl.ds(start, rows)], dst_ref=dslots.at[k], send_sem=rs_s.at[k],
            recv_sem=rs_r.at[k], device_id=(peers[k], grp), device_id_type=MESH,
        )

    def layer_copy(k):
        return pltpu.make_async_remote_copy(
            src_ref=zslots.at[layer], dst_ref=zslots.at[layer], send_sem=z_s.at[k],
            recv_sem=z_r.at[k], device_id=layers[k], device_id_type=MESH,
        )

    mine = pl.ds(pl.multiple_of(dom * rows, rows), rows)

    def spread_copy(k):
        return pltpu.make_async_remote_copy(
            src_ref=wfull.at[core, mine], dst_ref=wfull.at[core, mine], send_sem=ag_s.at[k],
            recv_sem=ag_r.at[k], device_id=(peers[k], grp), device_id_type=MESH,
        )

    halving.wait_recv()
    wsum[...] = (own + wsib[...].astype(F32)).astype(BF16)
    for k in order:
        scatter_copy(k).start()
    for k in order:
        gather_copy(k).start()

    out_ref[...] = (pre * sig).astype(BF16)
    stores = [
        pltpu.make_async_copy(out_ref, out_hbm, out_sem.at[0]),
        pltpu.make_async_copy(fg_ref, fg_hbm, out_sem.at[1]),
    ]
    stores[0].start()
    local_sum[...] = dot(dpre, ws_ref[...], 1, 1) + dot(dense_t[0], gsend[...])

    total = wsum[mine, :].astype(F32)
    for k in order:
        scatter_copy(k).wait_recv()
        total = total + dslots[k].astype(F32)
    zslots[layer] = total.astype(BF16)
    for k in range(depth - 1, 0, -1):
        layer_copy(k).start()
    for k in range(1, depth):
        layer_copy(k).wait_recv()
    total = zslots[0].astype(F32)
    for k in range(1, depth):
        total = total + zslots[k].astype(F32)
    wfull[core, mine, :] = (total * scale).astype(BF16)
    for k in order:
        spread_copy(k).start()
    finals = []

    def forward_piece(k):
        piece = wfull.at[core, pl.ds(pl.multiple_of(peers[k] * rows, rows), rows)]
        finals.append(sibling_copy(k, piece, piece))
        finals[-1].start()

    forward_piece(0)
    grad = local_sum[...]
    for k in order[::-1]:
        gather_copy(k).wait_recv()
        grad = grad + dot(dense_t[k], grecv[k])
    fg_ref[...] = grad.astype(BF16)
    stores[1].start()

    for k in order[::-1]:
        spread_copy(k).wait_recv()
        forward_piece(k)
    halves = [
        pltpu.make_async_copy(wg_ref.at[half], wg_hbm.at[half], out_sem.at[2 + i])
        for i, half in enumerate((core, 1 - core))
    ]
    wg_ref[core] = wfull[core].astype(F32)
    halves[0].start()
    for final in finals:
        final.wait_recv()
    wg_ref[1 - core] = wfull[1 - core].astype(F32)
    halves[1].start()
    halving.wait_send()
    for final in finals:
        final.wait_send()
    for k in order:
        forward_copy(k).wait_send()
        gather_copy(k).wait_send()
        scatter_copy(k).wait_send()
        spread_copy(k).wait_send()
    for k in range(1, depth):
        layer_copy(k).wait_send()
    for store in stores + halves:
        store.wait()


def finish(out_ref, fg_ref, wg_ref, out_hbm, fg_hbm, wg_hbm, out_v, fg_v, wg_v, in_sem, out_sem):
    trips = [
        (wg_ref.at[0], wg_v.at[0], wg_hbm.at[0]),
        (wg_ref.at[1], wg_v.at[1], wg_hbm.at[1]),
        (out_ref, out_v, out_hbm),
        (fg_ref, fg_v, fg_hbm),
    ]
    loads = [pltpu.make_async_copy(a, b, in_sem.at[i]) for i, (a, b, _) in enumerate(trips)]
    stores = [pltpu.make_async_copy(b, c, out_sem.at[i]) for i, (_, b, c) in enumerate(trips)]
    for load in loads:
        load.start()
    for load, store in zip(loads, stores):
        load.wait()
        store.start()
    for store in stores:
        store.wait()


def body(features, adjacency, src_tile, dst_peer, dst_tile, w_self, w_neigh, out_grad):
    nodes, width = features.shape
    parts, groups = lax.axis_size("dom"), lax.axis_size("grp")
    depth = groups // CORES
    scale = 1.0 / math.sqrt(nodes * parts * groups)
    rows = width // parts
    hbm = pl.BlockSpec(memory_space=pltpu.HBM)
    square = (nodes, width)
    dma = pltpu.SemaphoreType.DMA
    output, feat_grad, grads = pl.pallas_call(
        functools.partial(kernel, parts, depth, scale),
        out_shape=(
            jax.ShapeDtypeStruct(square, BF16),
            jax.ShapeDtypeStruct(square, BF16),
            jax.ShapeDtypeStruct((2, width, width), F32),
        ),
        in_specs=[hbm] * 8,
        out_specs=(hbm, hbm, hbm),
        scratch_shapes=[
            pltpu.SMEM(src_tile.shape, jnp.int32),
            pltpu.SMEM(src_tile.shape, jnp.int32),
            pltpu.SMEM(src_tile.shape, jnp.int32),
            pltpu.VMEM(square, BF16),
            pltpu.VMEM(adjacency.shape, BF16),
            pltpu.VMEM(w_self.shape, BF16),
            pltpu.VMEM(w_neigh.shape, BF16),
            pltpu.VMEM(square, BF16),
            pltpu.VMEM((parts, nodes, nodes), BF16),
            pltpu.VMEM((parts, nodes, nodes), BF16),
            pltpu.VMEM((parts,) + square, BF16),
            pltpu.VMEM((parts,) + square, BF16),
            pltpu.VMEM(square, BF16),
            pltpu.VMEM((parts,) + square, BF16),
            pltpu.VMEM((2, width, nodes), BF16),
            pltpu.VMEM((width, width), BF16),
            pltpu.VMEM((width, width), BF16),
            pltpu.VMEM((width, width), BF16),
            pltpu.VMEM((parts, rows, width), BF16),
            pltpu.VMEM((depth, rows, width), BF16),
            pltpu.VMEM((2, width, width), BF16),
            pltpu.VMEM(square, BF16),
            pltpu.VMEM(square, BF16),
            pltpu.VMEM((2, width, width), F32),
            pltpu.VMEM(square, F32),
            dma((8,)), dma((4,)), dma((parts,)), dma((parts,)), dma((parts,)), dma((parts,)),
            dma((parts + 1,)), dma((parts + 1,)), dma((parts,)), dma((parts,)),
            dma((depth,)), dma((depth,)), dma((parts,)), dma((parts,)),
        ],
        compiler_params=pltpu.CompilerParams(
            collective_id=0, has_side_effects=True, vmem_limit_bytes=VMEM_BYTES
        ),
        name="sage_layer",
    )(src_tile, dst_peer[:, 0], dst_tile, features, adjacency, w_self, w_neigh, out_grad)
    return pl.pallas_call(
        finish,
        out_shape=(
            jax.ShapeDtypeStruct(square, BF16),
            jax.ShapeDtypeStruct(square, BF16),
            jax.ShapeDtypeStruct((2, width, width), F32),
        ),
        in_specs=[hbm] * 3,
        out_specs=(hbm, hbm, hbm),
        scratch_shapes=[
            pltpu.VMEM(square, BF16),
            pltpu.VMEM(square, BF16),
            pltpu.VMEM((2, width, width), F32),
            dma((4,)), dma((4,)),
        ],
        compiler_params=pltpu.CompilerParams(vmem_limit_bytes=VMEM_BYTES),
        name="write_results",
    )(output, feat_grad, grads)


def solution(mesh):
    shard = ("dom", "grp")
    in_specs = (
        P(shard, None),
        P(shard, None, None),
        P(shard),
        P(shard, None),
        P(shard),
        P(),
        P(),
        P(shard, None),
    )
    out_specs = (P(shard, None), P(shard, None), P())
    return jax.shard_map(body, mesh=mesh, in_specs=in_specs, out_specs=out_specs, check_vma=False)
```

time: 56.3 us -> 31.4 us (0.56)
  Pallas kernels: 55.5 us -> 30.6 us
    pallas_call x1, Pallas kernels: 25 us -> 1.89 us  [body(): pl.pallas_call(finish, out_shape=(jax.ShapeDtypeStruct(square, BF16), jax...]
    pallas_call x1, Pallas kernels: 30.5 us -> 28.7 us  [body(): pl.pallas_call(functools.partial(kernel, parts, depth, scale), out_shape=...]
where the time goes in v3:
time: 31.4 us; the launch traced here: 31.2 us
  Pallas kernels  30.6 us (97%)
  between operations  0.64 us (2%)
    pallas_call x1, Pallas kernels, body(): pl.pallas_call(functools.partial(kernel, parts, depth, scale), out_shape=...  28.7 us
    pallas_call x1, Pallas kernels, body(): pl.pallas_call(finish, out_shape=(jax.ShapeDtypeStruct(square, BF16), jax...  1.89 us

profile of v3, /device:TPU:1, one launch (start us, length us, event | category | flops | bytes accessed | tf_op | source)
XLA Modules:
  0.0 31.2 jit_solution(4545736583617120593)
XLA Ops:
  0.6 28.7 %sage_layer.1 = (bf16[256,256]{1,0:T(8,128)(2,1)}, bf16[256,256]{1,0:T(8,128)(2,1)}, f32[2,256,256]{2,1,0:T(8,128)}) custom-call(s32[16]{0:T(128)} %src_hbm.1, s32[16]{0:T(128)} %bitcast.1, s32[16]{0:T(128)} %tile_hbm.1, bf16[256,256]{1,0:T(8,128)(2,1)} %x_hbm.1, bf16[16,128,128]{2,1,0:T(8,128)(2,1)} %adj_hbm.1, bf16[256,256]{1,0:T(8,128)(2,1)} %ws_hbm.1, ...), custom_call_target="tpu_custom_call" | custom-call | tf_op jit(solution)/shard_map/sage_layer/pallas_call | solution.py:264
  29.3 1.9 %write_results.1 = (bf16[256,256]{1,0:T(8,128)(2,1)}, bf16[256,256]{1,0:T(8,128)(2,1)}, f32[2,256,256]{2,1,0:T(8,128)}) custom-call(bf16[256,256]{1,0:T(8,128)(2,1)} %get-tuple-element.6.out_ref, bf16[256,256]{1,0:T(8,128)(2,1)} %get-tuple-element.7.fg_ref, f32[2,256,256]{2,1,0:T(8,128)} %get-tuple-element.8.wg_ref), custom_call_target="tpu_custom_call" | custom-call | tf_op jit(solution)/shard_map/write_results/pallas_call | solution.py:308

commit v4 on v3

--- a/solution.py
+++ b/solution.py
@@ -104,14 +104,66 @@
             device_id=(peers[k], grp), device_id_type=MESH,
         )
 
+    half = nodes // 2
+    lower, upper = pl.ds(0, half), pl.ds(half, half)
+
+    def hop(src, dst, i, send, recv, k):
+        return pltpu.make_async_remote_copy(
+            src_ref=src, dst_ref=dst, send_sem=send.at[i], recv_sem=recv.at[i],
+            device_id=(peers[k], grp), device_id_type=MESH,
+        )
+
+    relayed = parts == 4
+    if relayed:
+        forward_hops = [
+            hop(fsend.at[3, lower], frecv.at[3, lower], 0, fs_sem, fr_sem, 1),
+            hop(fsend.at[3, upper], frecv.at[3, upper], 1, fs_sem, fr_sem, 2),
+            hop(fsend.at[1, lower], frecv.at[1, lower], 2, fs_sem, fr_sem, 1),
+            hop(fsend.at[2, upper], frecv.at[2, upper], 3, fs_sem, fr_sem, 2),
+            hop(fsend.at[1, upper], frecv.at[1, upper], 4, fs_sem, fr_sem, 1),
+            hop(fsend.at[2, lower], frecv.at[2, lower], 5, fs_sem, fr_sem, 2),
+        ]
+        gather_hops = [
+            hop(gsend.at[lower], grecv.at[1, lower], 0, gs_sem, gr_sem, 1),
+            hop(gsend.at[upper], grecv.at[2, upper], 1, gs_sem, gr_sem, 2),
+            hop(gsend.at[upper], grecv.at[1, upper], 2, gs_sem, gr_sem, 1),
+            hop(gsend.at[lower], grecv.at[2, lower], 3, gs_sem, gr_sem, 2),
+            hop(grecv.at[2, upper], grecv.at[3, upper], 4, gs_sem, gr_sem, 1),
+            hop(grecv.at[1, lower], grecv.at[3, lower], 5, gs_sem, gr_sem, 2),
+        ]
+    else:
+        forward_hops = [forward_copy(k) for k in range(1, parts)]
+        gather_hops = [gather_copy(k) for k in range(1, parts)]
+
     x = x_ref[...]
     order = list(range(parts - 1, 0, -1))
-    for k in order:
-        build(k)
-        fsend[k] = dot(dense[k], x).astype(BF16)
-        if k == order[0]:
-            pl.semaphore_wait(barrier, len(partners))
-        forward_copy(k).start()
+    if relayed:
+        build(3)
+        fsend[3] = dot(dense[3], x).astype(BF16)
+        pl.semaphore_wait(barrier, len(partners))
+        forward_hops[0].start()
+        forward_hops[1].start()
+        build(1)
+        to_one = dot(dense[1], x)
+        fsend[1, :half] = to_one[:half].astype(BF16)
+        forward_hops[2].start()
+        build(2)
+        to_two = dot(dense[2], x)
+        fsend[2, half:] = to_two[half:].astype(BF16)
+        forward_hops[3].start()
+        forward_hops[1].wait_recv()
+        fsend[1, half:] = (to_one[half:] + frecv[3, half:].astype(F32)).astype(BF16)
+        forward_hops[4].start()
+        forward_hops[0].wait_recv()
+        fsend[2, :half] = (to_two[:half] + frecv[3, :half].astype(F32)).astype(BF16)
+        forward_hops[5].start()
+    else:
+        for k in order:
+            build(k)
+            fsend[k] = dot(dense[k], x).astype(BF16)
+            if k == order[0]:
+                pl.semaphore_wait(barrier, len(partners))
+            forward_hops[k - 1].start()
     build(0)
     for load in loads[5:]:
         load.wait()
@@ -120,9 +172,14 @@
     both_t[0] = x.T
     for k in range(parts):
         dense_t[k] = dense[k].T
-    for k in order:
-        forward_copy(k).wait_recv()
-        agg = agg + frecv[k].astype(F32)
+    if relayed:
+        for copy in forward_hops[2:]:
+            copy.wait_recv()
+        agg = agg + frecv[1].astype(F32) + frecv[2].astype(F32)
+    else:
+        for k in order:
+            forward_hops[k - 1].wait_recv()
+            agg = agg + frecv[k].astype(F32)
     agg_low = agg.astype(BF16)
     both_t[1] = agg_low.T
     pre = pre_self + dot(agg_low, wn_ref[...])
@@ -166,8 +223,8 @@
     wsum[...] = (own + wsib[...].astype(F32)).astype(BF16)
     for k in order:
         scatter_copy(k).start()
-    for k in order:
-        gather_copy(k).start()
+    for copy in gather_hops[:4] if relayed else gather_hops:
+        copy.start()
 
     out_ref[...] = (pre * sig).astype(BF16)
     stores = [
@@ -184,6 +241,11 @@
     zslots[layer] = total.astype(BF16)
     for k in range(depth - 1, 0, -1):
         layer_copy(k).start()
+    if relayed:
+        gather_hops[1].wait_recv()
+        gather_hops[4].start()
+        gather_hops[0].wait_recv()
+        gather_hops[5].start()
     for k in range(1, depth):
         layer_copy(k).wait_recv()
     total = zslots[0].astype(F32)
@@ -201,8 +263,9 @@
 
     forward_piece(0)
     grad = local_sum[...]
-    for k in order[::-1]:
-        gather_copy(k).wait_recv()
+    for copy in gather_hops[2:] if relayed else gather_hops:
+        copy.wait_recv()
+    for k in range(1, parts):
         grad = grad + dot(dense_t[k], grecv[k])
     fg_ref[...] = grad.astype(BF16)
     stores[1].start()
@@ -224,10 +287,10 @@
     for final in finals:
         final.wait_send()
     for k in order:
-        forward_copy(k).wait_send()
-        gather_copy(k).wait_send()
         scatter_copy(k).wait_send()
         spread_copy(k).wait_send()
+    for copy in forward_hops + gather_hops:
+        copy.wait_send()
     for k in range(1, depth):
         layer_copy(k).wait_send()
     for store in stores + halves:
@@ -258,6 +321,7 @@
     depth = groups // CORES
     scale = 1.0 / math.sqrt(nodes * parts * groups)
     rows = width // parts
+    hops = max(parts, 6)
     hbm = pl.BlockSpec(memory_space=pltpu.HBM)
     square = (nodes, width)
     dma = pltpu.SemaphoreType.DMA
@@ -296,7 +360,7 @@
             pltpu.VMEM(square, BF16),
             pltpu.VMEM((2, width, width), F32),
             pltpu.VMEM(square, F32),
-            dma((8,)), dma((4,)), dma((parts,)), dma((parts,)), dma((parts,)), dma((parts,)),
+            dma((8,)), dma((4,)), dma((hops,)), dma((hops,)), dma((hops,)), dma((hops,)),
             dma((parts + 1,)), dma((parts + 1,)), dma((parts,)), dma((parts,)),
             dma((depth,)), dma((depth,)), dma((parts,)), dma((parts,)),
         ],

time: 31.4 us -> 31.3 us (level)
  no operation moved by 1% of the time
where the time goes in v4:
time: 31.3 us; the launch traced here: 31.1 us
  Pallas kernels  30.5 us (97%)
  between operations  0.64 us (2%)
    pallas_call x1, Pallas kernels, body(): pl.pallas_call(functools.partial(kernel, parts, depth, scale), out_shape=...  28.6 us
    pallas_call x1, Pallas kernels, body(): pl.pallas_call(finish, out_shape=(jax.ShapeDtypeStruct(square, BF16), jax...  1.89 us

profile of v4, /device:TPU:1, one launch (start us, length us, event | category | flops | bytes accessed | tf_op | source)
XLA Modules:
  0.0 31.1 jit_solution(14023717003276085201)
XLA Ops:
  0.6 28.6 %sage_layer.1 = (bf16[256,256]{1,0:T(8,128)(2,1)}, bf16[256,256]{1,0:T(8,128)(2,1)}, f32[2,256,256]{2,1,0:T(8,128)}) custom-call(s32[16]{0:T(128)} %src_hbm.1, s32[16]{0:T(128)} %bitcast.1, s32[16]{0:T(128)} %tile_hbm.1, bf16[256,256]{1,0:T(8,128)(2,1)} %x_hbm.1, bf16[16,128,128]{2,1,0:T(8,128)(2,1)} %adj_hbm.1, bf16[256,256]{1,0:T(8,128)(2,1)} %ws_hbm.1, ...), custom_call_target="tpu_custom_call" | custom-call | tf_op jit(solution)/shard_map/sage_layer/pallas_call | solution.py:328
  29.2 1.9 %write_results.1 = (bf16[256,256]{1,0:T(8,128)(2,1)}, bf16[256,256]{1,0:T(8,128)(2,1)}, f32[2,256,256]{2,1,0:T(8,128)}) custom-call(bf16[256,256]{1,0:T(8,128)(2,1)} %get-tuple-element.6.out_ref, bf16[256,256]{1,0:T(8,128)(2,1)} %get-tuple-element.7.fg_ref, f32[2,256,256]{2,1,0:T(8,128)} %get-tuple-element.8.wg_ref), custom_call_target="tpu_custom_call" | custom-call | tf_op jit(solution)/shard_map/write_results/pallas_call | solution.py:372

commit v5 on v4

--- a/solution.py
+++ b/solution.py
@@ -11,7 +11,6 @@
 MESH = pl.DeviceIdType.MESH
 BF16 = jnp.bfloat16
 F32 = jnp.float32
-STRIP = 32
 CORES = 2
 VMEM_BYTES = 63 * 1024 * 1024
 
@@ -34,7 +33,7 @@
     src_hbm, peer_hbm, tile_hbm, x_hbm, adj_hbm, ws_hbm, wn_hbm, og_hbm,
     out_hbm, fg_hbm, wg_hbm,
     src_ref, peer_ref, tile_ref, x_ref, adj_ref, ws_ref, wn_ref, og_ref,
-    dense, dense_t, fsend, frecv, gsend, grecv, both_t, wsend, wsib, wsum, dslots, zslots, wfull, out_ref, fg_ref, wg_ref, local_sum,
+    runs, dense, dense_t, fsend, frecv, gsend, grecv, both_t, wsend, wsib, wsum, dslots, zslots, wfull, out_ref, fg_ref, wg_ref, local_sum,
     in_sem, out_sem, fs_sem, fr_sem, gs_sem, gr_sem, sib_s, sib_r, rs_s, rs_r, z_s, z_r, ag_s, ag_r,
 ):
     dom = lax.axis_index("dom")
@@ -66,31 +65,33 @@
     for partner in partners:
         pl.semaphore_signal(barrier, inc=1, device_id=partner, device_id_type=MESH)
 
-    for load in loads[:5]:
+    for load in loads[:3]:
         load.wait()
     codes = [(peer_ref[t] * nt + tile_ref[t]) * nt + src_ref[t] for t in range(count)]
+    earlier = []
+    for t in range(count):
+        slot = jnp.int32(0)
+        for u in range(t):
+            slot = jnp.where(codes[u] == codes[t], u + 1, slot)
+        earlier.append(slot)
+    latest = {}
+    for k in range(parts):
+        for c in range(nt * nt):
+            slot = jnp.int32(0)
+            for t in range(count):
+                slot = jnp.where(codes[t] == peers[k] * (nt * nt) + c, t + 1, slot)
+            latest[k, c] = slot
+    runs[0] = jnp.zeros((tile, tile), F32)
+    for load in loads[3:5]:
+        load.wait()
+    for t in range(count):
+        runs[t + 1] = runs[earlier[t]] + adj_ref[t].astype(F32)
 
     def build(k):
-        base = peers[k] * (nt * nt)
-        marks = [
-            [jnp.where(code - base == c, 1.0, 0.0).astype(F32) for c in range(nt * nt)]
-            for code in codes
-        ]
-
-        def strip(i, carry):
-            start = pl.multiple_of(i * STRIP, STRIP)
-            sums = [jnp.zeros((STRIP, tile), F32) for _ in range(nt * nt)]
-            for t in range(count):
-                block = adj_ref[t, pl.ds(start, STRIP), :].astype(F32)
-                for c in range(nt * nt):
-                    sums[c] = sums[c] + marks[t][c] * block
-            for c in range(nt * nt):
-                rows = pl.ds((c // nt) * tile + start, STRIP)
-                cols = pl.ds((c % nt) * tile, tile)
-                dense[k, rows, cols] = sums[c].astype(BF16)
-            return carry
-
-        lax.fori_loop(0, tile // STRIP, strip, 0)
+        for c in range(nt * nt):
+            rows_here = pl.ds((c // nt) * tile, tile)
+            cols_here = pl.ds((c % nt) * tile, tile)
+            dense[k, rows_here, cols_here] = runs[latest[k, c]].astype(BF16)
 
     def forward_copy(k):
         return pltpu.make_async_remote_copy(
@@ -317,6 +318,7 @@
 
 def body(features, adjacency, src_tile, dst_peer, dst_tile, w_self, w_neigh, out_grad):
     nodes, width = features.shape
+    count, tile = adjacency.shape[:2]
     parts, groups = lax.axis_size("dom"), lax.axis_size("grp")
     depth = groups // CORES
     scale = 1.0 / math.sqrt(nodes * parts * groups)
@@ -343,6 +345,7 @@
             pltpu.VMEM(w_self.shape, BF16),
             pltpu.VMEM(w_neigh.shape, BF16),
             pltpu.VMEM(square, BF16),
+            pltpu.VMEM((count + 1, tile, tile), F32),
             pltpu.VMEM((parts, nodes, nodes), BF16),
             pltpu.VMEM((parts, nodes, nodes), BF16),
             pltpu.VMEM((parts,) + square, BF16),

time: 31.3 us -> 31.1 us (level)
  no operation moved by 1% of the time
where the time goes in v5:
time: 31.1 us; the launch traced here: 30.9 us
  Pallas kernels  30.2 us (97%)
  between operations  0.64 us (2%)
    pallas_call x1, Pallas kernels, body(): pl.pallas_call(functools.partial(kernel, parts, depth, scale), out_shape=...  28.4 us
    pallas_call x1, Pallas kernels, body(): pl.pallas_call(finish, out_shape=(jax.ShapeDtypeStruct(square, BF16), jax...  1.89 us

profile of v5, /device:TPU:1, one launch (start us, length us, event | category | flops | bytes accessed | tf_op | source)
XLA Modules:
  0.0 30.9 jit_solution(10936155991214736669)
XLA Ops:
  0.6 28.4 %sage_layer.1 = (bf16[256,256]{1,0:T(8,128)(2,1)}, bf16[256,256]{1,0:T(8,128)(2,1)}, f32[2,256,256]{2,1,0:T(8,128)}) custom-call(s32[16]{0:T(128)} %src_hbm.1, s32[16]{0:T(128)} %bitcast.1, s32[16]{0:T(128)} %tile_hbm.1, bf16[256,256]{1,0:T(8,128)(2,1)} %x_hbm.1, bf16[16,128,128]{2,1,0:T(8,128)(2,1)} %adj_hbm.1, bf16[256,256]{1,0:T(8,128)(2,1)} %ws_hbm.1, ...), custom_call_target="tpu_custom_call" | custom-call | tf_op jit(solution)/shard_map/sage_layer/pallas_call | solution.py:330
  29.0 1.9 %write_results.1 = (bf16[256,256]{1,0:T(8,128)(2,1)}, bf16[256,256]{1,0:T(8,128)(2,1)}, f32[2,256,256]{2,1,0:T(8,128)}) custom-call(bf16[256,256]{1,0:T(8,128)(2,1)} %get-tuple-element.6.out_ref, bf16[256,256]{1,0:T(8,128)(2,1)} %get-tuple-element.7.fg_ref, f32[2,256,256]{2,1,0:T(8,128)} %get-tuple-element.8.wg_ref), custom_call_target="tpu_custom_call" | custom-call | tf_op jit(solution)/shard_map/write_results/pallas_call | solution.py:375

commit v6 on v5

--- a/solution.py
+++ b/solution.py
@@ -224,8 +224,6 @@
     wsum[...] = (own + wsib[...].astype(F32)).astype(BF16)
     for k in order:
         scatter_copy(k).start()
-    for copy in gather_hops[:4] if relayed else gather_hops:
-        copy.start()
 
     out_ref[...] = (pre * sig).astype(BF16)
     stores = [
@@ -242,6 +240,8 @@
     zslots[layer] = total.astype(BF16)
     for k in range(depth - 1, 0, -1):
         layer_copy(k).start()
+    for copy in gather_hops[:4] if relayed else gather_hops:
+        copy.start()
     if relayed:
         gather_hops[1].wait_recv()
         gather_hops[4].start()

time: 31.1 us -> 31.1 us (level)
  no operation moved by 1% of the time
where the time goes in v6:
time: 31.1 us; the launch traced here: 31 us
  Pallas kernels  30.3 us (97%)
  between operations  0.64 us (2%)
    pallas_call x1, Pallas kernels, body(): pl.pallas_call(functools.partial(kernel, parts, depth, scale), out_shape=...  28.4 us
    pallas_call x1, Pallas kernels, body(): pl.pallas_call(finish, out_shape=(jax.ShapeDtypeStruct(square, BF16), jax...  1.89 us

profile of v6, /device:TPU:1, one launch (start us, length us, event | category | flops | bytes accessed | tf_op | source)
XLA Modules:
  0.0 31.0 jit_solution(12202015513324924344)
XLA Ops:
  0.6 28.4 %sage_layer.1 = (bf16[256,256]{1,0:T(8,128)(2,1)}, bf16[256,256]{1,0:T(8,128)(2,1)}, f32[2,256,256]{2,1,0:T(8,128)}) custom-call(s32[16]{0:T(128)} %src_hbm.1, s32[16]{0:T(128)} %bitcast.1, s32[16]{0:T(128)} %tile_hbm.1, bf16[256,256]{1,0:T(8,128)(2,1)} %x_hbm.1, bf16[16,128,128]{2,1,0:T(8,128)(2,1)} %adj_hbm.1, bf16[256,256]{1,0:T(8,128)(2,1)} %ws_hbm.1, ...), custom_call_target="tpu_custom_call" | custom-call | tf_op jit(solution)/shard_map/sage_layer/pallas_call | solution.py:330
  29.1 1.9 %write_results.1 = (bf16[256,256]{1,0:T(8,128)(2,1)}, bf16[256,256]{1,0:T(8,128)(2,1)}, f32[2,256,256]{2,1,0:T(8,128)}) custom-call(bf16[256,256]{1,0:T(8,128)(2,1)} %get-tuple-element.6.out_ref, bf16[256,256]{1,0:T(8,128)(2,1)} %get-tuple-element.7.fg_ref, f32[2,256,256]{2,1,0:T(8,128)} %get-tuple-element.8.wg_ref), custom_call_target="tpu_custom_call" | custom-call | tf_op jit(solution)/shard_map/write_results/pallas_call | solution.py:375

commit v7 on v3

--- a/solution.py
+++ b/solution.py
@@ -11,7 +11,6 @@
 MESH = pl.DeviceIdType.MESH
 BF16 = jnp.bfloat16
 F32 = jnp.float32
-STRIP = 32
 CORES = 2
 VMEM_BYTES = 63 * 1024 * 1024
 
@@ -34,7 +33,7 @@
     src_hbm, peer_hbm, tile_hbm, x_hbm, adj_hbm, ws_hbm, wn_hbm, og_hbm,
     out_hbm, fg_hbm, wg_hbm,
     src_ref, peer_ref, tile_ref, x_ref, adj_ref, ws_ref, wn_ref, og_ref,
-    dense, dense_t, fsend, frecv, gsend, grecv, both_t, wsend, wsib, wsum, dslots, zslots, wfull, out_ref, fg_ref, wg_ref, local_sum,
+    runs, dense, dense_t, fsend, frecv, gsend, grecv, both_t, wsend, wsib, wsum, dslots, zslots, wfull, out_ref, fg_ref, wg_ref, local_sum,
     in_sem, out_sem, fs_sem, fr_sem, gs_sem, gr_sem, sib_s, sib_r, rs_s, rs_r, z_s, z_r, ag_s, ag_r,
 ):
     dom = lax.axis_index("dom")
@@ -66,31 +65,33 @@
     for partner in partners:
         pl.semaphore_signal(barrier, inc=1, device_id=partner, device_id_type=MESH)
 
-    for load in loads[:5]:
+    for load in loads[:3]:
         load.wait()
     codes = [(peer_ref[t] * nt + tile_ref[t]) * nt + src_ref[t] for t in range(count)]
+    earlier = []
+    for t in range(count):
+        slot = jnp.int32(0)
+        for u in range(t):
+            slot = jnp.where(codes[u] == codes[t], u + 1, slot)
+        earlier.append(slot)
+    latest = {}
+    for k in range(parts):
+        for c in range(nt * nt):
+            slot = jnp.int32(0)
+            for t in range(count):
+                slot = jnp.where(codes[t] == peers[k] * (nt * nt) + c, t + 1, slot)
+            latest[k, c] = slot
+    runs[0] = jnp.zeros((tile, tile), F32)
+    for load in loads[3:5]:
+        load.wait()
+    for t in range(count):
+        runs[t + 1] = runs[earlier[t]] + adj_ref[t].astype(F32)
 
     def build(k):
-        base = peers[k] * (nt * nt)
-        marks = [
-            [jnp.where(code - base == c, 1.0, 0.0).astype(F32) for c in range(nt * nt)]
-            for code in codes
-        ]
-
-        def strip(i, carry):
-            start = pl.multiple_of(i * STRIP, STRIP)
-            sums = [jnp.zeros((STRIP, tile), F32) for _ in range(nt * nt)]
-            for t in range(count):
-                block = adj_ref[t, pl.ds(start, STRIP), :].astype(F32)
-                for c in range(nt * nt):
-                    sums[c] = sums[c] + marks[t][c] * block
-            for c in range(nt * nt):
-                rows = pl.ds((c // nt) * tile + start, STRIP)
-                cols = pl.ds((c % nt) * tile, tile)
-                dense[k, rows, cols] = sums[c].astype(BF16)
-            return carry
-
-        lax.fori_loop(0, tile // STRIP, strip, 0)
+        for c in range(nt * nt):
+            rows_here = pl.ds((c // nt) * tile, tile)
+            cols_here = pl.ds((c % nt) * tile, tile)
+            dense[k, rows_here, cols_here] = runs[latest[k, c]].astype(BF16)
 
     def forward_copy(k):
         return pltpu.make_async_remote_copy(
@@ -120,7 +121,7 @@
     both_t[0] = x.T
     for k in range(parts):
         dense_t[k] = dense[k].T
-    for k in order:
+    for k in order[::-1]:
         forward_copy(k).wait_recv()
         agg = agg + frecv[k].astype(F32)
     agg_low = agg.astype(BF16)
@@ -139,6 +140,8 @@
     wsend[...] = dot(both_t[1 - core], dpre).astype(BF16)
     halving.start()
     gsend[...] = dot(dpre, wn_ref[...], 1, 1).astype(BF16)
+    for k in order:
+        gather_copy(k).start()
     own = dot(both_t[core], dpre)
 
     def scatter_copy(k):
@@ -166,8 +169,6 @@
     wsum[...] = (own + wsib[...].astype(F32)).astype(BF16)
     for k in order:
         scatter_copy(k).start()
-    for k in order:
-        gather_copy(k).start()
 
     out_ref[...] = (pre * sig).astype(BF16)
     stores = [
@@ -201,7 +202,7 @@
 
     forward_piece(0)
     grad = local_sum[...]
-    for k in order[::-1]:
+    for k in range(1, parts):
         gather_copy(k).wait_recv()
         grad = grad + dot(dense_t[k], grecv[k])
     fg_ref[...] = grad.astype(BF16)
@@ -224,10 +225,11 @@
     for final in finals:
         final.wait_send()
     for k in order:
+        scatter_copy(k).wait_send()
+        spread_copy(k).wait_send()
+    for k in order:
         forward_copy(k).wait_send()
         gather_copy(k).wait_send()
-        scatter_copy(k).wait_send()
-        spread_copy(k).wait_send()
     for k in range(1, depth):
         layer_copy(k).wait_send()
     for store in stores + halves:
@@ -254,6 +256,7 @@
 
 def body(features, adjacency, src_tile, dst_peer, dst_tile, w_self, w_neigh, out_grad):
     nodes, width = features.shape
+    count, tile = adjacency.shape[:2]
     parts, groups = lax.axis_size("dom"), lax.axis_size("grp")
     depth = groups // CORES
     scale = 1.0 / math.sqrt(nodes * parts * groups)
@@ -279,6 +282,7 @@
             pltpu.VMEM(w_self.shape, BF16),
             pltpu.VMEM(w_neigh.shape, BF16),
             pltpu.VMEM(square, BF16),
+            pltpu.VMEM((count + 1, tile, tile), F32),
             pltpu.VMEM((parts, nodes, nodes), BF16),
             pltpu.VMEM((parts, nodes, nodes), BF16),
             pltpu.VMEM((parts,) + square, BF16),

time: 31.4 us -> 35 us (1.11)
  Pallas kernels: 30.6 us -> 34.2 us
    pallas_call x1, Pallas kernels: 28.7 us -> 32.3 us  [body(): pl.pallas_call(functools.partial(kernel, parts, depth, scale), out_shape=...]
where the time goes in v7:
time: 35 us; the launch traced here: 34.8 us
  Pallas kernels  34.2 us (98%)
  between operations  0.64 us (2%)
    pallas_call x1, Pallas kernels, body(): pl.pallas_call(functools.partial(kernel, parts, depth, scale), out_shape=...  32.3 us
    pallas_call x1, Pallas kernels, body(): pl.pallas_call(finish, out_shape=(jax.ShapeDtypeStruct(square, BF16), jax...  1.89 us

profile of v7, /device:TPU:1, one launch (start us, length us, event | category | flops | bytes accessed | tf_op | source)
XLA Modules:
  0.0 34.8 jit_solution(9083282794552445477)
XLA Ops:
  0.6 32.3 %sage_layer.1 = (bf16[256,256]{1,0:T(8,128)(2,1)}, bf16[256,256]{1,0:T(8,128)(2,1)}, f32[2,256,256]{2,1,0:T(8,128)}) custom-call(s32[16]{0:T(128)} %src_hbm.1, s32[16]{0:T(128)} %bitcast.1, s32[16]{0:T(128)} %tile_hbm.1, bf16[256,256]{1,0:T(8,128)(2,1)} %x_hbm.1, bf16[16,128,128]{2,1,0:T(8,128)(2,1)} %adj_hbm.1, bf16[256,256]{1,0:T(8,128)(2,1)} %ws_hbm.1, ...), custom_call_target="tpu_custom_call" | custom-call | tf_op jit(solution)/shard_map/sage_layer/pallas_call | solution.py:267
  33.0 1.9 %write_results.1 = (bf16[256,256]{1,0:T(8,128)(2,1)}, bf16[256,256]{1,0:T(8,128)(2,1)}, f32[2,256,256]{2,1,0:T(8,128)}) custom-call(bf16[256,256]{1,0:T(8,128)(2,1)} %get-tuple-element.6.out_ref, bf16[256,256]{1,0:T(8,128)(2,1)} %get-tuple-element.7.fg_ref, f32[2,256,256]{2,1,0:T(8,128)} %get-tuple-element.8.wg_ref), custom_call_target="tpu_custom_call" | custom-call | tf_op jit(solution)/shard_map/write_results/pallas_call | solution.py:312

commit v8 on v5

--- a/solution.py
+++ b/solution.py
@@ -206,18 +206,26 @@
             recv_sem=rs_r.at[k], device_id=(peers[k], grp), device_id_type=MESH,
         )
 
-    def layer_copy(k):
-        return pltpu.make_async_remote_copy(
-            src_ref=zslots.at[layer], dst_ref=zslots.at[layer], send_sem=z_s.at[k],
-            recv_sem=z_r.at[k], device_id=layers[k], device_id_type=MESH,
+    pieces = 2 if rows % 32 == 0 else 1
+    part = rows // pieces
+
+    def layer_copy(k, p):
+        place = zslots.at[layer, pl.ds(p * part, part)]
+        return pltpu.make_async_remote_copy(
+            src_ref=place, dst_ref=place, send_sem=z_s.at[p * depth + k],
+            recv_sem=z_r.at[p * depth + k], device_id=layers[k], device_id_type=MESH,
         )
 
     mine = pl.ds(pl.multiple_of(dom * rows, rows), rows)
 
-    def spread_copy(k):
-        return pltpu.make_async_remote_copy(
-            src_ref=wfull.at[core, mine], dst_ref=wfull.at[core, mine], send_sem=ag_s.at[k],
-            recv_sem=ag_r.at[k], device_id=(peers[k], grp), device_id_type=MESH,
+    def own_part(p):
+        return pl.ds(pl.multiple_of(dom * rows + p * part, part), part)
+
+    def spread_copy(k, p):
+        place = wfull.at[core, own_part(p)]
+        return pltpu.make_async_remote_copy(
+            src_ref=place, dst_ref=place, send_sem=ag_s.at[p * parts + k],
+            recv_sem=ag_r.at[p * parts + k], device_id=(peers[k], grp), device_id_type=MESH,
         )
 
     halving.wait_recv()
@@ -240,21 +248,24 @@
         scatter_copy(k).wait_recv()
         total = total + dslots[k].astype(F32)
     zslots[layer] = total.astype(BF16)
-    for k in range(depth - 1, 0, -1):
-        layer_copy(k).start()
+    for p in range(pieces):
+        for k in range(depth - 1, 0, -1):
+            layer_copy(k, p).start()
     if relayed:
         gather_hops[1].wait_recv()
         gather_hops[4].start()
         gather_hops[0].wait_recv()
         gather_hops[5].start()
-    for k in range(1, depth):
-        layer_copy(k).wait_recv()
-    total = zslots[0].astype(F32)
-    for k in range(1, depth):
-        total = total + zslots[k].astype(F32)
-    wfull[core, mine, :] = (total * scale).astype(BF16)
-    for k in order:
-        spread_copy(k).start()
+    for p in range(pieces):
+        for k in range(1, depth):
+            layer_copy(k, p).wait_recv()
+        here = pl.ds(p * part, part)
+        total = zslots[0, here].astype(F32)
+        for k in range(1, depth):
+            total = total + zslots[k, here].astype(F32)
+        wfull[core, own_part(p), :] = (total * scale).astype(BF16)
+        for k in order:
+            spread_copy(k, p).start()
     finals = []
 
     def forward_piece(k):
@@ -272,7 +283,8 @@
     stores[1].start()
 
     for k in order[::-1]:
-        spread_copy(k).wait_recv()
+        for p in range(pieces):
+            spread_copy(k, p).wait_recv()
         forward_piece(k)
     halves = [
         pltpu.make_async_copy(wg_ref.at[half], wg_hbm.at[half], out_sem.at[2 + i])
@@ -289,11 +301,13 @@
         final.wait_send()
     for k in order:
         scatter_copy(k).wait_send()
-        spread_copy(k).wait_send()
+        for p in range(pieces):
+            spread_copy(k, p).wait_send()
     for copy in forward_hops + gather_hops:
         copy.wait_send()
     for k in range(1, depth):
-        layer_copy(k).wait_send()
+        for p in range(pieces):
+            layer_copy(k, p).wait_send()
     for store in stores + halves:
         store.wait()
 
@@ -365,7 +379,7 @@
             pltpu.VMEM(square, F32),
             dma((8,)), dma((4,)), dma((hops,)), dma((hops,)), dma((hops,)), dma((hops,)),
             dma((parts + 1,)), dma((parts + 1,)), dma((parts,)), dma((parts,)),
-            dma((depth,)), dma((depth,)), dma((parts,)), dma((parts,)),
+            dma((2 * depth,)), dma((2 * depth,)), dma((2 * parts,)), dma((2 * parts,)),
         ],
         compiler_params=pltpu.CompilerParams(
             collective_id=0, has_side_effects=True, vmem_limit_bytes=VMEM_BYTES

time: 31.1 us -> 30.7 us (0.987)
    pallas_call x1, Pallas kernels: 28.4 us -> 28 us  [body(): pl.pallas_call(functools.partial(kernel, parts, depth, scale), out_shape=...]
where the time goes in v8:
time: 30.7 us; the launch traced here: 30.5 us
  Pallas kernels  29.9 us (97%)
  between operations  0.64 us (2%)
    pallas_call x1, Pallas kernels, body(): pl.pallas_call(functools.partial(kernel, parts, depth, scale), out_shape=...  28 us
    pallas_call x1, Pallas kernels, body(): pl.pallas_call(finish, out_shape=(jax.ShapeDtypeStruct(square, BF16), jax...  1.89 us

profile of v8, /device:TPU:1, one launch (start us, length us, event | category | flops | bytes accessed | tf_op | source)
XLA Modules:
  0.0 30.5 jit_solution(2089985440739616260)
XLA Ops:
  0.6 28.0 %sage_layer.1 = (bf16[256,256]{1,0:T(8,128)(2,1)}, bf16[256,256]{1,0:T(8,128)(2,1)}, f32[2,256,256]{2,1,0:T(8,128)}) custom-call(s32[16]{0:T(128)} %src_hbm.1, s32[16]{0:T(128)} %bitcast.1, s32[16]{0:T(128)} %tile_hbm.1, bf16[256,256]{1,0:T(8,128)(2,1)} %x_hbm.1, bf16[16,128,128]{2,1,0:T(8,128)(2,1)} %adj_hbm.1, bf16[256,256]{1,0:T(8,128)(2,1)} %ws_hbm.1, ...), custom_call_target="tpu_custom_call" | custom-call | tf_op jit(solution)/shard_map/sage_layer/pallas_call | solution.py:344
  28.6 1.9 %write_results.1 = (bf16[256,256]{1,0:T(8,128)(2,1)}, bf16[256,256]{1,0:T(8,128)(2,1)}, f32[2,256,256]{2,1,0:T(8,128)}) custom-call(bf16[256,256]{1,0:T(8,128)(2,1)} %get-tuple-element.6.out_ref, bf16[256,256]{1,0:T(8,128)(2,1)} %get-tuple-element.7.fg_ref, f32[2,256,256]{2,1,0:T(8,128)} %get-tuple-element.8.wg_ref), custom_call_target="tpu_custom_call" | custom-call | tf_op jit(solution)/shard_map/write_results/pallas_call | solution.py:389
